TPU v7x, 32 devices: a whole 2x2x4 slice. The times are simulated.
32 devices in a mesh: groups: 2 (over y), wt: 4 (over z), dp: 2 (over x), lin: 2 (over core).
Axes of the slice: x: 2, y: 2, z: 4, core: 2. Of those that a mesh axis runs over, the one named last changes fastest.
Arguments:
- weights: bfloat16 [4, 8192, 8192], P(('groups', 'lin'), 'dp', 'wt'), parts along dimension 0
- codes: int32 [4, 8192, 8192], P(('groups', 'lin'), 'dp', 'wt'), parts along dimension 0, may hold values from 0 to 15, as said below
- scales: float32 [4, 64, 8192], P(('groups', 'lin'), 'wt', 'dp'), parts along dimension 0, may hold values from 0.5 to 5
- tokens: bfloat16 [4096, 8192], P(('groups', 'dp'), 'wt'), parts along dimension 0, may hold values from -6 to 6
- sketch: bfloat16 [4096, 256], P(('groups', 'dp')), parts along dimension 0, may hold values from -6 to 6
Outputs:
- basis: float32 [4, 8192, 256], P(('groups', 'lin'), ('dp', 'wt')), parts along dimension 0
- factor: float32 [4, 8192, 256], P(('groups', 'lin'), 'wt'), parts along dimension 0
There are 2 independent parts, one for each index of `groups`. A program takes and returns all parts, laid end to end along the dimension named above; each array names one. Nothing has to cross between parts.
Inputs may be any that keep to these rules, and one draw needn't show every extreme that they name: codes holds the int4 codes of weights under scales: weights lies within about half a scale of s (codes - 8).
All inputs are finite; a program needn't handle non-finite values.
Results may differ from a plain program's by a relative error of at most 0.03.
Values may be sent and summed in bfloat16 or wider, within the bound.
A program may use at most 192 MiB of HBM per device.

v0:
```python
import math

import jax
import jax.numpy as jnp
from jax import lax
from jax.sharding import PartitionSpec as P

OUT = 8192
G = 128
ITERS = 1


def cross(left, right):
    return lax.dot_general(
        left, right, (((0,), (0,)), ((), ())), preferred_element_type=jnp.float32
    )


def local(weights, codes, scales, tokens, sketch):
    expanded = jnp.repeat(scales[0], G, axis=0).T
    error = (
        weights[0].astype(jnp.float32) - expanded * (codes[0].astype(jnp.float32) - 8.0)
    ).astype(jnp.bfloat16)

    def token_moment(vectors):
        return lax.psum(cross(tokens, vectors), "dp").astype(jnp.bfloat16)

    moment = token_moment(sketch)
    projected = None
    lower = None
    image_share = None
    for step in range(ITERS + 1):
        current = moment
        image_share = lax.psum_scatter(
            jnp.dot(error, current, preferred_element_type=jnp.float32),
            "wt",
            scatter_dimension=0,
            tiled=True,
        ).astype(jnp.bfloat16)
        gram = lax.psum(cross(image_share, image_share), ("wt", "dp"))
        partial_panel = cross(error, lax.all_gather(image_share, "wt", axis=0, tiled=True))
        panel = lax.psum(partial_panel, "dp")
        lower = jnp.linalg.cholesky(gram)
        projected = jax.scipy.linalg.solve_triangular(lower, panel.T, lower=True).T
        if step < ITERS:
            rounded = projected.astype(jnp.bfloat16)
            scores = lax.psum(jnp.dot(tokens, rounded, preferred_element_type=jnp.float32), "wt")
            moment = token_moment(scores.astype(jnp.bfloat16))
    basis = jax.scipy.linalg.solve_triangular(
        lower, image_share.astype(jnp.float32).T, lower=True
    ).T * math.sqrt(OUT)
    return (basis[None], projected[None])


def solution(mesh):
    placed = (
        P(("groups", "lin"), "dp", "wt"),
        P(("groups", "lin"), "dp", "wt"),
        P(("groups", "lin"), "wt", "dp"),
        P(("groups", "dp"), "wt"),
        P(("groups", "dp"), None),
    )
    return jax.shard_map(
        local,
        mesh=mesh,
        in_specs=placed,
        out_specs=(P(("groups", "lin"), ("dp", "wt"), None), P(("groups", "lin"), "wt", None)),
        check_vma=False,
    )
```

profile of v0, /device:TPU:0, one launch (start us, length us, event | category | flops | bytes accessed | tf_op | source)
XLA Modules:
  0.0 793.0 jit_solution(4822395431555781843)
XLA Ops:
  7.2 1.6 copy.7
  8.8 4.8 fusion.36
  13.7 55.1 %all-reduce.16 = bf16[2048,256]{1,0:T(8,128)(2,1)} all-reduce(f32[2048,256]{1,0:T(8,128)} %fusion.36), channel_id=1, replica_groups=mesh['groups'=2,'wt'=4,'dp'=2,'lin'=2] {'dp'}, use_global_device_ids=true, to_apply=%region_0.0 | all-reduce | flops 524288 | bytes 3145728 | tf_op jit(solution)/shard_map/psum | solution.py:26
  68.7 16.9 %broadcast_in_dim.10 = f32[16,128,4096]{1,0,2:T(8,128)} broadcast(f32[16,4096]{0,1:T(8,128)S(1)} %copy.7), dimensions={0,2} | broadcast | bytes 33816576 | tf_op jit(solution)/shard_map/broadcast_in_dim | solution.py:20
  85.6 29.5 %fusion.2 = bf16[4096,2048]{1,0:T(8,128)(2,1)S(1)} fusion(f32[512,8,16,128]{3,2,1,0:T(8,128)} %bitcast.127, s32[1,4096,2048]{2,1,0:T(8,128)} %param.9, bf16[1,4096,2048]{2,1,0:T(8,128)(2,1)} %param.8), kind=kLoop, calls=%fused_computation.7 | loop fusion | flops 50331648 | bytes 100663296 | tf_op jit(solution)/shard_map/convert_element_type | solution.py:23
  115.1 5.7 copy-done.2
  120.8 6.0 fusion.42
  126.9 77.2 %reduce-scatter.3.cloned.1.call-done = f32[1024,256]{1,0:T(8,128)} async-done(((f32[4096,256]{1,0:T(8,128)}), f32[1024,256]{1,0:T(8,128)}) %reduce-scatter.3.cloned.1.call-update) | async-done | bytes 1048592 | tf_op jit(solution)/shard_map/reduce_scatter | solution.py:34
  204.1 2.1 convert_element_type.38
  206.2 2.4 fusion.37
  208.7 44.1 %all-gather.3.cloned.1.call-done = bf16[4096,256]{1,0:T(8,128)(2,1)} async-done(((bf16[1024,256]{1,0:T(8,128)(2,1)}), bf16[4096,256]{1,0:T(8,128)(2,1)}) %all-gather.3.cloned.1.call-update) | async-done | bytes 2097168 | tf_op jit(solution)/shard_map/all_gather | solution.py:41
  252.8 12.2 %fusion.38 = f32[256,2048]{1,0:T(8,128)} fusion(bf16[4096,256]{1,0:T(8,128)(2,1)} %all-gather.3.cloned.1.call-done, bf16[4096,2048]{1,0:T(8,128)(2,1)} %copy-done.2), kind=kOutput, calls=%fused_computation.77 | convolution fusion | flops 4294967296 | bytes 20971520 | tf_op jit(solution)/shard_map/dot_general | solution.py:14
  265.1 0.5 reduce-scatter.5.cloned.1.call-start
  265.6 60.2 %all-reduce.9.cloned.1.call-done = f32[256,256]{0,1:T(8,128)} async-done(((f32[256,256]{0,1:T(8,128)}), f32[256,256]{0,1:T(8,128)}) %all-reduce.9.cloned.1.call-update) | async-done | bytes 262160 | tf_op jit(solution)/shard_map/psum | solution.py:40
  325.8 1.1 copy.9
  326.9 1.0 fusion.16
  327.9 11.7 %cholesky.130 = f32[128,128]{1,0:T(8,128)S(1)} custom-call(f32[128,128]{1,0:T(8,128)S(1)} %cholesky.194), custom_call_target="Cholesky" | custom-call | tf_op jit(solution)/shard_map/jit(cholesky)/cholesky | solution.py:43
  339.7 9.8 %custom-call.18 = f32[1,128,128]{1,2,0:T(8,128)S(1)} custom-call(f32[1,128,128]{2,1,0:T(8,128)S(1)} %get-tuple-element.57), custom_call_target="InvertDiagBlocksLowerTriangular" | custom-call | tf_op jit(solution)/shard_map/jit(cholesky)/cholesky | solution.py:43
  350.0 11.7 %cholesky.147 = f32[128,128]{1,0:T(8,128)S(1)} custom-call(f32[128,128]{1,0:T(8,128)S(1)} %convolution_subtract_fusion.4), custom_call_target="Cholesky" | custom-call | tf_op jit(solution)/shard_map/jit(cholesky)/cholesky | solution.py:43
  361.7 0.7 compare_reduce_fusion.2
  363.8 4.1 while.6
  364.0 0.6 fusion.73
  364.6 1.3 bitcast_dynamic-update-slice_fusion.5
  365.9 0.6 fusion.73
  366.5 1.3 bitcast_dynamic-update-slice_fusion.5
  367.9 19.7 %custom-call.19 = f32[2,128,128]{1,2,0:T(8,128)S(1)} custom-call(f32[2,128,128]{2,1,0:T(8,128)S(1)} %get-tuple-element.26), custom_call_target="InvertDiagBlocksLowerTriangular" | custom-call | tf_op jit(solution)/shard_map/jit(_solve_triangular)/triangular_solve | solution.py:44
  387.6 3.4 all-reduce.11.cloned.1.call-done
  391.0 2.4 fusion.5
  393.4 2.2 convolution_subtract_fusion.1
  395.6 1.1 fusion.20
  396.7 1.3 convolution_bitcast_fusion.1
  398.0 43.3 %all-reduce.17 = bf16[1024,256]{0,1:T(8,128)(2,1)S(1)} all-reduce(f32[1024,256]{0,1:T(8,128)S(1)} %convolution_bitcast_fusion.1), channel_id=1, replica_groups=mesh['groups'=2,'wt'=4,'dp'=2,'lin'=2] {'wt'}, use_global_device_ids=true, to_apply=%region_8.0 | all-reduce | flops 262144 | bytes 1572864 | tf_op jit(solution)/shard_map/psum | solution.py:47
  441.3 3.4 convolution_bitcast_fusion
  444.8 48.0 %all-reduce.18 = bf16[2048,256]{0,1:T(8,128)(2,1)} all-reduce(f32[2048,256]{0,1:T(8,128)S(1)} %convolution_bitcast_fusion), channel_id=1, replica_groups=mesh['groups'=2,'wt'=4,'dp'=2,'lin'=2] {'dp'}, use_global_device_ids=true, to_apply=%region_9.12 | all-reduce | flops 524288 | bytes 3145728 | tf_op jit(solution)/shard_map/psum | solution.py:26
  492.7 12.5 %fusion.41 = f32[4096,256]{1,0:T(8,128)} fusion(bf16[4096,2048]{1,0:T(8,128)(2,1)} %copy-done.2, bf16[2048,256]{0,1:T(8,128)(2,1)} %all-reduce.18), kind=kOutput, calls=%fused_computation.80 | convolution fusion | flops 4294967296 | bytes 22020096 | tf_op jit(solution)/shard_map/dot_general | solution.py:35
  505.3 75.7 %reduce-scatter.5.cloned.1.call-done = f32[1024,256]{1,0:T(8,128)} async-done(((f32[4096,256]{1,0:T(8,128)}), f32[1024,256]{1,0:T(8,128)}) %reduce-scatter.5.cloned.1.call-update) | async-done | bytes 1048592 | tf_op jit(solution)/shard_map/reduce_scatter | solution.py:34
  581.0 1.4 convert_element_type.42
  582.4 1.1 fusion.39
  583.5 0.7 all-gather.5.cloned.1.call-update
  584.6 71.4 %all-reduce.13.cloned.1.call-done = f32[256,256]{0,1:T(8,128)} async-done(((f32[256,256]{0,1:T(8,128)}), f32[256,256]{0,1:T(8,128)}) %all-reduce.13.cloned.1.call-update) | async-done | bytes 262160 | tf_op jit(solution)/shard_map/psum | solution.py:40
  655.9 1.1 copy.11
  657.0 1.0 fusion.15
  658.0 11.7 %cholesky.164 = f32[128,128]{1,0:T(8,128)S(1)} custom-call(f32[128,128]{1,0:T(8,128)S(1)} %cholesky.197), custom_call_target="Cholesky" | custom-call | tf_op jit(solution)/shard_map/jit(cholesky)/cholesky | solution.py:43
  669.8 9.8 %custom-call.20 = f32[1,128,128]{1,2,0:T(8,128)S(1)} custom-call(f32[1,128,128]{2,1,0:T(8,128)S(1)} %get-tuple-element.53), custom_call_target="InvertDiagBlocksLowerTriangular" | custom-call | tf_op jit(solution)/shard_map/jit(cholesky)/cholesky | solution.py:43
  680.1 11.7 %cholesky.181 = f32[128,128]{1,0:T(8,128)S(1)} custom-call(f32[128,128]{1,0:T(8,128)S(1)} %convolution_subtract_fusion.3), custom_call_target="Cholesky" | custom-call | tf_op jit(solution)/shard_map/jit(cholesky)/cholesky | solution.py:43
  691.8 11.4 %all-gather.5.cloned.1.call-done = bf16[4096,256]{1,0:T(8,128)(2,1)} async-done(((bf16[1024,256]{1,0:T(8,128)(2,1)}), bf16[4096,256]{1,0:T(8,128)(2,1)}) %all-gather.5.cloned.1.call-update) | async-done | bytes 2097168 | tf_op jit(solution)/shard_map/all_gather | solution.py:41
  703.2 12.5 %fusion.40 = f32[256,2048]{1,0:T(8,128)} fusion(bf16[4096,256]{1,0:T(8,128)(2,1)} %all-gather.5.cloned.1.call-done, bf16[4096,2048]{1,0:T(8,128)(2,1)} %copy-done.2), kind=kOutput, calls=%fused_computation.79 | convolution fusion | flops 4294967296 | bytes 20971520 | tf_op jit(solution)/shard_map/dot_general | solution.py:14
  715.8 0.6 compare_reduce_fusion
  716.4 0.6 compare_reduce_fusion.1
  718.4 4.0 while.5
  718.4 0.6 fusion.72
  719.0 1.4 bitcast_dynamic-update-slice_fusion.4
  720.4 0.6 fusion.72
  721.0 1.4 bitcast_dynamic-update-slice_fusion.4
  722.3 19.7 %custom-call.15 = f32[2,128,128]{1,2,0:T(8,128)S(1)} custom-call(f32[2,128,128]{2,1,0:T(8,128)S(1)} %get-tuple-element.19), custom_call_target="InvertDiagBlocksLowerTriangular" | custom-call | tf_op jit(solution)/shard_map/jit(_solve_triangular)/triangular_solve | solution.py:49
  742.0 0.4 fusion.13
  742.4 1.0 convolution_subtract_fusion.2
  743.4 0.6 fusion.30
  744.2 1.3 copy.12
  745.5 32.6 %all-reduce.15.cloned.1.call-done = f32[256,2048]{1,0:T(8,128)} async-done(((f32[256,2048]{1,0:T(8,128)}), f32[256,2048]{1,0:T(8,128)}) %all-reduce.15.cloned.1.call-update) | async-done | bytes 2097168 | tf_op jit(solution)/shard_map/psum | solution.py:42
  778.1 2.3 fusion.3
  780.4 2.2 convolution_subtract_fusion
  782.7 1.1 fusion.29
  783.9 1.8 copy.13
  (52 shorter events, 2.3 us)
Async XLA Ops:
  7.2 1.7 copy-start
  7.2 196.9 %reduce-scatter.3.cloned.1.call-start = ((), (), s32[]{:S(2)}) async-start(), calls=%async_computation.2 | async-start | bytes 5242880 | tf_op jit(solution)/shard_map/reduce_scatter | solution.py:34
  85.6 35.2 %copy-start.5 = (bf16[2048,256]{1,0:T(8,128)(2,1)S(1)}, bf16[2048,256]{1,0:T(8,128)(2,1)}, u32[]{:S(2)}) copy-start(bf16[2048,256]{1,0:T(8,128)(2,1)} %all-reduce.16) | copy-start | bytes 3145732
  115.1 5.7 copy-start.2
  126.9 125.9 %all-gather.3.cloned.1.call-start = ((), (), s32[]{:S(2)}) async-start(), calls=%async_computation.4 | async-start | bytes 2621440 | tf_op jit(solution)/shard_map/all_gather | solution.py:41
  206.2 119.6 %all-reduce.9.cloned.1.call-start = ((), (), s32[]{:S(2)}) async-start(), calls=%async_computation.3 | async-start | bytes 524288 | tf_op jit(solution)/shard_map/psum | solution.py:40
  208.7 182.3 %all-reduce.11.cloned.1.call-start = ((), (), s32[]{:S(2)}) async-start(), calls=%async_computation.5 | async-start | bytes 4194304 | tf_op jit(solution)/shard_map/psum | solution.py:42
  265.1 316.0 %reduce-scatter.5.cloned.1.call-start = ((), (), s32[]{:S(2)}) async-start(), calls=%async_computation.6 | async-start | bytes 5242880 | tf_op jit(solution)/shard_map/reduce_scatter | solution.py:34
  391.0 5.7 copy-start.6
  505.3 150.7 %all-reduce.13.cloned.1.call-start = ((), (), s32[]{:S(2)}) async-start(), calls=%async_computation.7 | async-start | bytes 524288 | tf_op jit(solution)/shard_map/psum | solution.py:40
  581.0 3.5 copy-start.4
  582.4 1.1 copy-start.3
  583.5 119.7 %all-gather.5.cloned.1.call-start = ((), (), s32[]{:S(2)}) async-start(), calls=%async_computation.8 | async-start | bytes 2621440 | tf_op jit(solution)/shard_map/all_gather | solution.py:41
  584.2 193.9 %all-reduce.15.cloned.1.call-start = ((), (), s32[]{:S(2)}) async-start(), calls=%async_computation.9 | async-start | bytes 4194304 | tf_op jit(solution)/shard_map/psum | solution.py:42
  782.7 3.0 copy-start.1
Sparse Core Ops, SparseCore 0:
  127.0 77.0 reduce-scatter.2
  206.3 46.4 all-gather.2
  256.5 69.2 all-reduce.8
  328.5 62.3 all-reduce.10
  505.4 75.5 reduce-scatter.4
  584.8 71.0 all-reduce.12
  658.2 45.0 all-gather.4
  715.9 62.2 all-reduce.14
where the time goes:
time: 802 us; the launch traced here: 793 us
  waiting for transfers between devices  377 us (47%)
  blocking collectives  146 us (18%)
  other arithmetic  143 us (18%)
  matrix products  70.5 us (9%)
  local copies, waits for them, and re-layouts  37.4 us (5%)
  between operations  17.4 us (2%)
    reduce_scatter x2, waiting for transfers between devices, local(): lax.psum_scatter(jnp.dot(error, current, preferred_element_type=jnp.float...  153 us
    psum x2, waiting for transfers between devices, local(): gram = lax.psum(cross(image_share, image_share), ('wt', 'dp'))  132 us
    psum x2, blocking collectives, token_moment(): return lax.psum(cross(tokens, vectors), 'dp').astype(jnp.bfloat16)  103 us
    another operation x13, other arithmetic, local(): lower = jnp.linalg.cholesky(gram)  68.6 us
    all_gather x2, waiting for transfers between devices, local(): lax.all_gather(image_share, 'wt', axis=0, tiled=True)  55.5 us
    psum x1, blocking collectives, local(): lax.psum(jnp.dot(tokens, rounded, preferred_element_type=jnp.float32), 'wt')  43.3 us
    dot_general x6, matrix products, cross(): lax.dot_general(left, right, (((0,), (0,)), ((), ())), preferred_element_...  36.5 us
    psum x2, waiting for transfers between devices, local(): panel = lax.psum(partial_panel, 'dp')  36 us
  transfers between devices with their start and end apart: 8, of which 8 were waited for; matrix products, arithmetic and copies ran while one was open for 18% of the time, Pallas kernels for 0%

commit v1 on v0

v1 whole, which is shorter than its diff:
```python
import functools
import math

import jax
import jax.numpy as jnp
from jax import lax
from jax.experimental import pallas as pl
from jax.experimental.pallas import tpu as pltpu
from jax.sharding import PartitionSpec as P

OUT = 8192
G = 128
ITERS = 1
HIGHEST = lax.Precision.HIGHEST


def cross(left, right):
    return lax.dot_general(
        left, right, (((0,), (0,)), ((), ())), preferred_element_type=jnp.float32
    )


def error_kernel(w_ref, c_ref, s_ref, e_ref):
    scale = s_ref[...]
    for g in range(w_ref.shape[1] // G):
        cols = slice(g * G, (g + 1) * G)
        step = scale[:, g : g + 1] * (c_ref[:, cols].astype(jnp.float32) - 8.0)
        e_ref[:, cols] = (w_ref[:, cols].astype(jnp.float32) - step).astype(jnp.bfloat16)


def quant_error(weights, codes, scales):
    rows, cols = weights.shape
    tile = 256
    return pl.pallas_call(
        error_kernel,
        grid=(rows // tile,),
        in_specs=[
            pl.BlockSpec((tile, cols), lambda i: (i, 0)),
            pl.BlockSpec((tile, cols), lambda i: (i, 0)),
            pl.BlockSpec((tile, cols // G), lambda i: (i, 0)),
        ],
        out_specs=pl.BlockSpec((tile, cols), lambda i: (i, 0)),
        out_shape=jax.ShapeDtypeStruct((rows, cols), jnp.bfloat16),
        compiler_params=pltpu.CompilerParams(vmem_limit_bytes=32 * 2**20),
        cost_estimate=pl.CostEstimate(
            flops=4 * rows * cols, bytes_accessed=8 * rows * cols, transcendentals=0
        ),
        name="quant_error",
    )(weights, codes, scales.T)


def invert_block(a):
    n = a.shape[0]
    lane = lax.broadcasted_iota(jnp.int32, (8, n), 1)
    sub = lax.broadcasted_iota(jnp.int32, (8, n), 0)
    blocks = [a[8 * b : 8 * b + 8, :] for b in range(n // 8)]
    for j in range(n):
        home, r = divmod(j, 8)
        row = blocks[home][r : r + 1, :]
        pivot = jnp.broadcast_to(row[:, j : j + 1], (8, n))
        line = jnp.broadcast_to(row, (8, n))
        line = jnp.where(lane == j, 1.0, line) / pivot
        for b in range(home, n // 8):
            if b == home and r == 7:
                continue
            col = jnp.broadcast_to(blocks[b][:, j : j + 1], (8, n))
            new = jnp.where(lane == j, 0.0, blocks[b]) - col * line
            blocks[b] = jnp.where(sub > r, new, blocks[b]) if b == home else new
    out = []
    for b in range(n // 8):
        index = sub + 8 * b
        diag = jnp.sum(jnp.where(lane == index, blocks[b], 0.0), axis=1, keepdims=True)
        unit = jnp.where(lane < index, blocks[b], jnp.where(lane == index, 1.0, 0.0))
        out.append(unit * lax.rsqrt(diag))
    return jnp.concatenate(out, axis=0)


def dot_hi(left, right, dims):
    return lax.dot_general(
        left, right, (dims, ((), ())), precision=HIGHEST, preferred_element_type=jnp.float32
    )


def invert_kernel(a_ref, o_ref):
    n = a_ref.shape[0]
    h = n // 2
    top = invert_block(a_ref[:h, :h])
    low = dot_hi(a_ref[h:, :h], top, ((1,), (1,)))
    rest = a_ref[h:, h:] - dot_hi(low, low, ((1,), (1,)))
    bottom = invert_block(rest)
    o_ref[:h, :h] = top
    o_ref[:h, h:] = jnp.zeros((h, h), jnp.float32)
    o_ref[h:, h:] = bottom
    o_ref[h:, :h] = -dot_hi(bottom, dot_hi(low, top, ((1,), (0,))), ((1,), (0,)))


def inverse_factor(gram):
    n = gram.shape[0]
    return pl.pallas_call(
        invert_kernel,
        out_shape=jax.ShapeDtypeStruct((n, n), jnp.float32),
        compiler_params=pltpu.CompilerParams(vmem_limit_bytes=16 * 2**20),
        cost_estimate=pl.CostEstimate(
            flops=40 * 10**9, bytes_accessed=2 * 4 * n * n, transcendentals=0
        ),
        name="inverse_factor",
    )(gram)


def local(dp, weights, codes, scales, tokens, sketch):
    pairs = [(i, (i + s) % dp) for s in range(1, dp) for i in range(dp)]

    def dp_sum(part):
        if dp == 2:
            other = lax.ppermute(part, "dp", pairs)
            return part.astype(jnp.float32) + other.astype(jnp.float32)
        return lax.psum(part.astype(jnp.float32), "dp")

    def token_moment(vectors):
        part = cross(tokens, vectors).astype(jnp.bfloat16)
        return dp_sum(part).astype(jnp.bfloat16)

    moment = token_moment(sketch)
    error = quant_error(weights[0], codes[0], scales[0])
    rounded = None
    projected = None
    for step in range(ITERS + 1):
        part = jnp.dot(error, moment, preferred_element_type=jnp.float32).astype(jnp.bfloat16)
        share = lax.psum_scatter(part, "wt", scatter_dimension=0, tiled=True)
        image = lax.all_gather(share, "wt", axis=0, tiled=True)
        gram = dp_sum(cross(image, image))
        panel = dp_sum(cross(error, image).astype(jnp.bfloat16))
        inverse = inverse_factor(gram)
        projected = dot_hi(panel, inverse, ((1,), (1,)))
        if step < ITERS:
            rounded = projected.astype(jnp.bfloat16)
            scores = jnp.dot(tokens, rounded, preferred_element_type=jnp.float32)
            scores = lax.psum(scores.astype(jnp.bfloat16), "wt")
            moment = token_moment(scores)
    basis = dot_hi(share.astype(jnp.float32), inverse * math.sqrt(OUT), ((1,), (1,)))
    return (basis[None], projected[None])


def solution(mesh):
    placed = (
        P(("groups", "lin"), "dp", "wt"),
        P(("groups", "lin"), "dp", "wt"),
        P(("groups", "lin"), "wt", "dp"),
        P(("groups", "dp"), "wt"),
        P(("groups", "dp"), None),
    )
    return jax.shard_map(
        functools.partial(local, mesh.shape["dp"]),
        mesh=mesh,
        in_specs=placed,
        out_specs=(P(("groups", "lin"), ("dp", "wt"), None), P(("groups", "lin"), "wt", None)),
        check_vma=False,
    )
```

time: 802 us -> 440 us (0.55)
  blocking collectives: 146 us -> 0 us
  other arithmetic: 143 us -> 0.07 us
  waiting for transfers between devices: 377 us -> 241 us
  Pallas kernels: 0 us -> 92.9 us
  local copies, waits for them, and re-layouts: 37.4 us -> 7.34 us
    psum x3 -> x0, blocking collectives: 146 us -> none  [the longest x2 103 us: token_moment(): return lax.psum(cross(tokens, vectors), 'dp').astype(jnp.bfloat16)]
    psum x4 -> x1, waiting for transfers between devices: 168 us -> 37.1 us  [local(): scores = lax.psum(scores.astype(jnp.bfloat16), 'wt')]
    another operation x18 -> x0, other arithmetic: 108 us -> none  [the longest x13 68.6 us: local(): lower = jnp.linalg.cholesky(gram)]
    pallas_call x0 -> x3, Pallas kernels: none -> 92.9 us  [the longest x2 70.2 us: inverse_factor(): pl.pallas_call(invert_kernel, out_shape=jax.ShapeDtypeStruct((n, n), jnp....]
    reduce_scatter x2, waiting for transfers between devices: 153 us -> 87.9 us  [local(): share = lax.psum_scatter(part, 'wt', scatter_dimension=0, tiled=True)]
    all_gather x2, waiting for transfers between devices: 55.5 us -> 93.5 us  [local(): image = lax.all_gather(share, 'wt', axis=0, tiled=True)]
    convert_element_type x3 -> x0, other arithmetic: 33 us -> none  [the longest x1 29.5 us: local(): error = (weights[0].astype(jnp.float32) - expanded * (codes[0].astype(jnp...]
    ppermute x0 -> x6, waiting for transfers between devices: none -> 22.5 us  [dp_sum(): other = lax.ppermute(part, 'dp', pairs)]
  transfers between devices with their start and end apart: 8 -> 11, of which waited for: 8 -> 6; matrix products, arithmetic and copies ran while one was open for 18% -> 4% of each run, Pallas kernels for 0% -> 21%
where the time goes in v1:
time: 440 us; the launch traced here: 438 us
  waiting for transfers between devices  241 us (55%)
  Pallas kernels  92.9 us (21%)
  matrix products  73.1 us (17%)
  between operations  14.1 us (3%)
  starting transfers between devices  8.99 us (2%)
  local copies, waits for them, and re-layouts  7.34 us (2%)
    all_gather x2, waiting for transfers between devices, local(): image = lax.all_gather(share, 'wt', axis=0, tiled=True)  93.5 us
    reduce_scatter x2, waiting for transfers between devices, local(): share = lax.psum_scatter(part, 'wt', scatter_dimension=0, tiled=True)  87.9 us
    pallas_call x2, Pallas kernels, inverse_factor(): pl.pallas_call(invert_kernel, out_shape=jax.ShapeDtypeStruct((n, n), jnp....  70.2 us
    psum x1, waiting for transfers between devices, local(): scores = lax.psum(scores.astype(jnp.bfloat16), 'wt')  37.1 us
    dot_general x2, matrix products, local(): jnp.dot(error, moment, preferred_element_type=jnp.float32)  32.8 us
    dot_general x6, matrix products, cross(): lax.dot_general(left, right, (((0,), (0,)), ((), ())), preferred_element_...  31.5 us
    pallas_call x1, Pallas kernels, quant_error(): pl.pallas_call(error_kernel, grid=(rows // tile,), in_specs=[pl.BlockSpec...  22.7 us
    ppermute x6, waiting for transfers between devices, dp_sum(): other = lax.ppermute(part, 'dp', pairs)  22.5 us
  transfers between devices with their start and end apart: 11, of which 6 were waited for; matrix products, arithmetic and copies ran while one was open for 4% of the time, Pallas kernels for 21%

profile of v1, /device:TPU:0, one launch (start us, length us, event | category | flops | bytes accessed | tf_op | source)
XLA Modules:
  0.0 437.6 jit_solution(577461441189104971)
XLA Ops:
  7.2 0.0 copy-start
  7.2 0.0 copy-start.4
  7.2 0.0 reduce-scatter.3.cloned.1.call-start
  7.2 1.0 copy-done
  8.2 4.5 %convolution_convert_fusion.6 = bf16[2048,256]{1,0:T(8,128)(2,1)} fusion(bf16[1024,2048]{1,0:T(8,128)(2,1)} %param.8, bf16[1024,256]{1,0:T(8,128)(2,1)S(1)} %copy-done), kind=kOutput, calls=%fused_computation.7 | convolution fusion | flops 1074266112 | bytes 5767168 | tf_op jit(solution)/shard_map/dot_general | solution.py:18
  12.7 2.9 collective-permute-start
  15.6 0.0 copy-done.4
  15.7 0.6 copy.7
  16.3 22.7 %quant_error.1 = bf16[4096,2048]{1,0:T(8,128)(2,1)S(1)} custom-call(bf16[4096,2048]{1,0:T(8,128)(2,1)} %bitcast.34, s32[4096,2048]{1,0:T(8,128)} %bitcast.33, f32[4096,16]{1,0:T(8,128)S(1)} %bitcast.32), custom_call_target="tpu_custom_call" | custom-call | flops 33554432 | bytes 67108864 | tf_op jit(solution)/shard_map/quant_error/pallas_call | solution.py:34
  39.0 0.0 copy-start.2
  39.0 5.7 %copy-done.2 = bf16[4096,2048]{1,0:T(8,128)(2,1)} copy-done((bf16[4096,2048]{1,0:T(8,128)(2,1)}, bf16[4096,2048]{1,0:T(8,128)(2,1)S(1)}, u32[]{:S(2)}) %copy-start.2) | copy-done | bytes 16777240
  44.7 0.0 collective-permute-done
  44.7 12.2 %convolution_convert_fusion.1 = bf16[4096,256]{1,0:T(8,128)(2,1)} fusion(bf16[4096,2048]{1,0:T(8,128)(2,1)} %copy-done.2, bf16[2048,256]{1,0:T(8,128)(2,1)} %collective-permute-done, bf16[2048,256]{1,0:T(8,128)(2,1)} %convolution_convert_fusion.6), kind=kOutput, calls=%fused_computation.1 | convolution fusion | flops 4298113024 | bytes 20971520 | tf_op jit(solution)/shard_map/dot_general | solution.py:128
  56.9 0.0 reduce-scatter.3.cloned.1.call-update
  56.9 0.0 all-gather.3.cloned.1.call-start
  57.0 44.3 %reduce-scatter.3.cloned.1.call-done = bf16[1024,256]{1,0:T(8,128)(2,1)} async-done(((bf16[4096,256]{1,0:T(8,128)(2,1)}), bf16[1024,256]{1,0:T(8,128)(2,1)}) %reduce-scatter.3.cloned.1.call-update) | async-done | bytes 524304 | tf_op jit(solution)/shard_map/reduce_scatter | solution.py:129
  101.3 0.0 all-gather.3.cloned.1.call-update
  101.3 0.0 all-reduce.2.cloned.1.call-start
  101.3 46.9 %all-gather.3.cloned.1.call-done = bf16[4096,256]{1,0:T(8,128)(2,1)} async-done(((bf16[1024,256]{1,0:T(8,128)(2,1)}), bf16[4096,256]{1,0:T(8,128)(2,1)}) %all-gather.3.cloned.1.call-update) | async-done | bytes 2097168 | tf_op jit(solution)/shard_map/all_gather | solution.py:130
  148.2 0.0 copy-start.6
  148.2 3.1 fusion.11
  151.3 1.5 collective-permute-start.2
  152.8 0.0 copy-done.6
  152.9 8.7 %convolution_convert_fusion.4 = bf16[2048,256]{1,0:T(8,128)(2,1)S(1)} fusion(bf16[4096,2048]{1,0:T(8,128)(2,1)} %copy-done.2, bf16[4096,256]{1,0:T(8,128)(2,1)S(1)} %copy-done.6), kind=kOutput, calls=%fused_computation.5 | convolution fusion | flops 4295491584 | bytes 19922944 | tf_op jit(solution)/shard_map/dot_general | solution.py:18
  161.6 0.6 collective-permute-start.1
  162.2 0.0 collective-permute-done.2
  162.3 0.0 copy-start.5
  162.3 35.1 %inverse_factor.2 = f32[256,256]{1,0:T(8,128)S(1)} custom-call(f32[256,256]{1,0:T(8,128)S(1)} %add.26.a_ref), custom_call_target="tpu_custom_call" | custom-call | flops 40000000000 | bytes 524288 | tf_op jit(solution)/shard_map/inverse_factor/pallas_call | solution.py:99
  197.4 0.0 collective-permute-done.1
  197.4 1.9 convolution_convert_fusion.3
  199.3 0.0 copy-done.5
  199.3 2.1 fusion.7
  201.4 0.0 all-reduce.2.cloned.1.call-update
  201.4 0.0 reduce-scatter.5.cloned.1.call-start
  201.5 37.1 %all-reduce.2.cloned.1.call-done = bf16[1024,256]{0,1:T(8,128)(2,1)} async-done(((bf16[1024,256]{0,1:T(8,128)(2,1)}), bf16[1024,256]{0,1:T(8,128)(2,1)}) %all-reduce.2.cloned.1.call-update) | async-done | bytes 524304 | tf_op jit(solution)/shard_map/psum | solution.py:138
  238.6 3.6 fusion
  242.2 1.5 collective-permute-start.3
  243.7 22.5 %collective-permute-done.3 = bf16[2048,256]{0,1:T(8,128)(2,1)S(1)} collective-permute-done((bf16[2048,256]{0,1:T(8,128)(2,1)S(1)}, bf16[2048,256]{0,1:T(8,128)(2,1)S(1)}, u32[]{:S(2)}, u32[]{:S(2)}) %collective-permute-start.3) | collective-permute-done | bytes 1048608 | tf_op jit(solution)/shard_map/ppermute | solution.py:115
  266.2 20.6 %convolution_convert_fusion = bf16[4096,256]{1,0:T(8,128)(2,1)} fusion(bf16[4096,2048]{1,0:T(8,128)(2,1)} %copy-done.2, bf16[2048,256]{0,1:T(8,128)(2,1)S(1)} %collective-permute-done.3, bf16[2048,256]{0,1:T(8,128)(2,1)S(1)} %fusion), kind=kOutput, calls=%fused_computation | convolution fusion | flops 4298113024 | bytes 20971520 | tf_op jit(solution)/shard_map/dot_general | solution.py:128
  286.7 0.0 reduce-scatter.5.cloned.1.call-update
  286.8 0.0 all-gather.5.cloned.1.call-start
  286.8 43.6 %reduce-scatter.5.cloned.1.call-done = bf16[1024,256]{1,0:T(8,128)(2,1)} async-done(((bf16[4096,256]{1,0:T(8,128)(2,1)}), bf16[1024,256]{1,0:T(8,128)(2,1)}) %reduce-scatter.5.cloned.1.call-update) | async-done | bytes 524304 | tf_op jit(solution)/shard_map/reduce_scatter | solution.py:129
  330.4 0.0 all-gather.5.cloned.1.call-update
  330.4 46.7 %all-gather.5.cloned.1.call-done = bf16[4096,256]{1,0:T(8,128)(2,1)} async-done(((bf16[1024,256]{1,0:T(8,128)(2,1)}), bf16[4096,256]{1,0:T(8,128)(2,1)}) %all-gather.5.cloned.1.call-update) | async-done | bytes 2097168 | tf_op jit(solution)/shard_map/all_gather | solution.py:130
  377.1 0.0 copy-start.7
  377.1 3.1 fusion.12
  380.2 1.5 collective-permute-start.4
  381.8 0.0 copy-done.7
  381.8 8.5 %convolution_convert_fusion.2 = bf16[2048,256]{1,0:T(8,128)(2,1)S(1)} fusion(bf16[4096,2048]{1,0:T(8,128)(2,1)} %copy-done.2, bf16[4096,256]{1,0:T(8,128)(2,1)S(1)} %copy-done.7), kind=kOutput, calls=%fused_computation.3 | convolution fusion | flops 4295491584 | bytes 19922944 | tf_op jit(solution)/shard_map/dot_general | solution.py:18
  390.3 0.6 collective-permute-start.5
  390.9 0.0 collective-permute-done.4
  390.9 0.0 copy-start.3
  390.9 35.1 %inverse_factor.3 = f32[256,256]{1,0:T(8,128)S(1)} custom-call(f32[256,256]{1,0:T(8,128)S(1)} %add.28.a_ref), custom_call_target="tpu_custom_call" | custom-call | flops 40000000000 | bytes 524288 | tf_op jit(solution)/shard_map/inverse_factor/pallas_call | solution.py:99
  426.0 0.0 copy-done.3
  426.1 0.0 copy-start.1
  426.1 1.6 convolution_bitcast_fusion.1
  427.7 0.0 collective-permute-done.5
  427.7 3.2 convolution_bitcast_fusion
  430.9 0.0 copy-done.1
  (2 shorter events, 0.1 us)
Async XLA Ops:
  7.2 1.1 copy-start
  7.2 8.5 %copy-start.4 = (f32[1,16,4096]{2,1,0:T(8,128)S(1)}, f32[1,16,4096]{2,1,0:T(8,128)}, u32[]{:S(2)}) copy-start(f32[1,16,4096]{2,1,0:T(8,128)} %param.7) | copy-start | bytes 786436
  7.2 94.1 %reduce-scatter.3.cloned.1.call-start = ((), (), s32[]{:S(2)}) async-start(), calls=%async_computation.2 | async-start | bytes 2621440 | tf_op jit(solution)/shard_map/reduce_scatter | solution.py:129
  12.7 32.0 %collective-permute-start = (bf16[2048,256]{1,0:T(8,128)(2,1)}, bf16[2048,256]{1,0:T(8,128)(2,1)}, u32[]{:S(2)}, u32[]{:S(2)}) collective-permute-start(bf16[2048,256]{1,0:T(8,128)(2,1)} %convolution_convert_fusion.6), channel_id=1, source_target_pairs={{0,2},{2,0},{1,3},{3,1},{4,6},{6,4},{5,7},{7,5},{8,10},{10,8},{9,1... | collective-permute-start | bytes 3145736 | tf_op jit(solution)/shard_map/ppermute | solution.py:115
  39.0 5.7 %copy-start.2 = (bf16[4096,2048]{1,0:T(8,128)(2,1)}, bf16[4096,2048]{1,0:T(8,128)(2,1)S(1)}, u32[]{:S(2)}) copy-start(bf16[4096,2048]{1,0:T(8,128)(2,1)S(1)} %quant_error.1) | copy-start | bytes 50331652
  56.9 91.3 %all-gather.3.cloned.1.call-start = ((), (), s32[]{:S(2)}) async-start(), calls=%async_computation.3 | async-start | bytes 2621440 | tf_op jit(solution)/shard_map/all_gather | solution.py:130
  101.3 137.3 %all-reduce.2.cloned.1.call-start = ((), (), s32[]{:S(2)}) async-start(), calls=%async_computation.4 | async-start | bytes 1048576 | tf_op jit(solution)/shard_map/psum | solution.py:138
  148.2 4.7 %copy-start.6 = (bf16[4096,256]{1,0:T(8,128)(2,1)S(1)}, bf16[4096,256]{1,0:T(8,128)(2,1)}, u32[]{:S(2)}) copy-start(bf16[4096,256]{1,0:T(8,128)(2,1)} %all-gather.3.cloned.1.call-done) | copy-start | bytes 6291460
  151.3 10.9 %collective-permute-start.2 = (f32[256,256]{1,0:T(8,128)S(1)}, f32[256,256]{1,0:T(8,128)S(1)}, u32[]{:S(2)}, u32[]{:S(2)}) collective-permute-start(f32[256,256]{1,0:T(8,128)S(1)} %fusion.11), channel_id=1, source_target_pairs={{0,2},{2,0},{1,3},{3,1},{4,6},{6,4},{5,7},{7,5},{8,10},{10,8},{9,1... | collective-permute-start | bytes 786440 | tf_op jit(solution)/shard_map/ppermute | solution.py:115
  161.6 35.8 %collective-permute-start.1 = (bf16[2048,256]{1,0:T(8,128)(2,1)S(1)}, bf16[2048,256]{1,0:T(8,128)(2,1)S(1)}, u32[]{:S(2)}, u32[]{:S(2)}) collective-permute-start(bf16[2048,256]{1,0:T(8,128)(2,1)S(1)} %convolution_convert_fusion.4), channel_id=1, source_target_pairs={{0,2},{2,0},{1,3},{3,1},{4,6},{6,4},{5,7},{7,5},{8,10},{10,8},{9,1... | collective-permute-start | bytes 3145736 | tf_op jit(solution)/shard_map/ppermute | solution.py:115
  162.3 37.0 %copy-start.5 = (bf16[1024,2048]{1,0:T(8,128)(2,1)S(1)}, bf16[1024,2048]{1,0:T(8,128)(2,1)}, u32[]{:S(2)}) copy-start(bf16[1024,2048]{1,0:T(8,128)(2,1)} %param.8) | copy-start | bytes 12582916
  201.4 129.0 %reduce-scatter.5.cloned.1.call-start = ((), (), s32[]{:S(2)}) async-start(), calls=%async_computation.5 | async-start | bytes 2621440 | tf_op jit(solution)/shard_map/reduce_scatter | solution.py:129
  242.2 24.0 %collective-permute-start.3 = (bf16[2048,256]{0,1:T(8,128)(2,1)S(1)}, bf16[2048,256]{0,1:T(8,128)(2,1)S(1)}, u32[]{:S(2)}, u32[]{:S(2)}) collective-permute-start(bf16[2048,256]{0,1:T(8,128)(2,1)S(1)} %fusion), channel_id=1, source_target_pairs={{0,2},{2,0},{1,3},{3,1},{4,6},{6,4},{5,7},{7,5},{8,10},{10,8},{9,1... | collective-permute-start | bytes 3145736 | tf_op jit(solution)/shard_map/ppermute | solution.py:115
  286.8 90.3 %all-gather.5.cloned.1.call-start = ((), (), s32[]{:S(2)}) async-start(), calls=%async_computation.6 | async-start | bytes 2621440 | tf_op jit(solution)/shard_map/all_gather | solution.py:130
  377.1 4.7 %copy-start.7 = (bf16[4096,256]{1,0:T(8,128)(2,1)S(1)}, bf16[4096,256]{1,0:T(8,128)(2,1)}, u32[]{:S(2)}) copy-start(bf16[4096,256]{1,0:T(8,128)(2,1)} %all-gather.5.cloned.1.call-done) | copy-start | bytes 6291460
  380.2 10.7 %collective-permute-start.4 = (f32[256,256]{1,0:T(8,128)S(1)}, f32[256,256]{1,0:T(8,128)S(1)}, u32[]{:S(2)}, u32[]{:S(2)}) collective-permute-start(f32[256,256]{1,0:T(8,128)S(1)} %fusion.12), channel_id=1, source_target_pairs={{0,2},{2,0},{1,3},{3,1},{4,6},{6,4},{5,7},{7,5},{8,10},{10,8},{9,1... | collective-permute-start | bytes 786440 | tf_op jit(solution)/shard_map/ppermute | solution.py:115
  390.3 37.4 %collective-permute-start.5 = (bf16[2048,256]{1,0:T(8,128)(2,1)S(1)}, bf16[2048,256]{1,0:T(8,128)(2,1)S(1)}, u32[]{:S(2)}, u32[]{:S(2)}) collective-permute-start(bf16[2048,256]{1,0:T(8,128)(2,1)S(1)} %convolution_convert_fusion.2), channel_id=1, source_target_pairs={{0,2},{2,0},{1,3},{3,1},{4,6},{6,4},{5,7},{7,5},{8,10},{10,8},{9,1... | collective-permute-start | bytes 3145736 | tf_op jit(solution)/shard_map/ppermute | solution.py:115
  390.9 35.1 %copy-start.3 = (bf16[1024,256]{1,0:T(8,128)(2,1)S(1)}, bf16[1024,256]{1,0:T(8,128)(2,1)}, u32[]{:S(2)}) copy-start(bf16[1024,256]{1,0:T(8,128)(2,1)} %reduce-scatter.5.cloned.1.call-done) | copy-start | bytes 1572868
  426.1 4.8 %copy-start.1 = (bf16[1024,256]{1,0:T(8,128)(2,1)S(1)}, bf16[1024,256]{1,0:T(8,128)(2,1)}, u32[]{:S(2)}) copy-start(bf16[1024,256]{1,0:T(8,128)(2,1)} %param.9) | copy-start | bytes 1572868
Sparse Core Ops, SparseCore 0:
  57.0 44.1 reduce-scatter.2
  102.9 45.2 all-gather.2
  201.5 36.9 all-reduce.1
  286.9 43.4 reduce-scatter.4
  331.8 45.2 all-gather.4

commit v2 on v1

--- a/solution.py
+++ b/solution.py
@@ -107,7 +107,166 @@
     )(gram)
 
 
-def local(dp, weights, codes, scales, tokens, sketch):
+PIECES = 16
+
+
+def image_kernel(
+    e_ref, m_ref, image_ref, panel_ref, gram_ref,
+    stage, outer_in, inner_in, final, total,
+    s_part, r_outer, s_in, r_in, s_fin_in, s_fin_out, r_fin,
+):
+    me = lax.axis_index("wt")
+    half = PIECES // 2
+    size = e_ref.shape[0] // PIECES
+    low = me < 2
+    is_end = (me == 0) | (me == 3)
+    middle = jnp.where(low, 1, 2)
+    outer = jnp.where(low, 0, 3)
+    inner = jnp.where(low, 2, 1)
+    mine = jnp.where(low, 0, half)
+    other = half - mine
+    barrier = pltpu.get_barrier_semaphore()
+
+    def rows(p):
+        return pl.ds(pl.multiple_of(p * size, size), size)
+
+    def copy(src, dst, send, recv, target):
+        return pltpu.make_async_remote_copy(
+            src_ref=src, dst_ref=dst, send_sem=send, recv_sem=recv,
+            device_id={"wt": target}, device_id_type=pl.DeviceIdType.MESH,
+        )
+
+    def part_copy(p):
+        return copy(stage.at[p], outer_in.at[p], s_part.at[p], r_outer.at[p], middle)
+
+    def in_copy(p, k):
+        return copy(stage.at[p], inner_in.at[k], s_in.at[k], r_in.at[k], inner)
+
+    def fin_in_copy(p, k):
+        return copy(final.at[p], final.at[p], s_fin_in.at[k], r_fin.at[p], inner)
+
+    def fin_out_copy(p, target):
+        return copy(final.at[p], final.at[p], s_fin_out.at[p], r_fin.at[p], target)
+
+    def own(p):
+        return jnp.dot(e_ref[rows(p), :], m_ref[...], preferred_element_type=jnp.float32)
+
+    def consume(p):
+        piece = final[p]
+        image_ref[rows(p), :] = piece
+        total[...] += cross(piece, e_ref[rows(p), :])
+        gram_ref[...] += cross(piece, piece)
+
+    def greet(target):
+        pl.semaphore_signal(
+            barrier, inc=1, device_id={"wt": target}, device_id_type=pl.DeviceIdType.MESH
+        )
+
+    total[...] = jnp.zeros_like(total)
+    gram_ref[...] = jnp.zeros_like(gram_ref)
+
+    @pl.when(is_end)
+    def _():
+        greet(middle)
+        pl.semaphore_wait(barrier, 1)
+
+        @pl.loop(0, PIECES)
+        def _(t):
+            p = jnp.where(lax.rem(t, 2) == 0, other, mine) + lax.div(t, 2)
+            stage[p] = own(p).astype(jnp.bfloat16)
+            part_copy(p).start()
+
+        @pl.loop(0, PIECES)
+        def _(t):
+            p = jnp.where(lax.rem(t, 2) == 0, mine, other) + lax.div(t, 2)
+            fin_out_copy(p, middle).wait_recv()
+            consume(p)
+
+        @pl.loop(0, PIECES)
+        def _(p):
+            part_copy(p).wait_send()
+
+    @pl.when(jnp.logical_not(is_end))
+    def _():
+        greet(outer)
+        greet(inner)
+        pl.semaphore_wait(barrier, 2)
+
+        def forward(k):
+            o = other + k
+            fin_in_copy(o, k).wait_recv()
+            fin_out_copy(o, outer).start()
+            consume(o)
+
+        @pl.loop(0, half)
+        def _(k):
+            o, m = other + k, mine + k
+            left = own(o)
+            part_copy(o).wait_recv()
+            stage[o] = (left + outer_in[o].astype(jnp.float32)).astype(jnp.bfloat16)
+            in_copy(o, k).start()
+            left = own(m)
+            part_copy(m).wait_recv()
+            left = left + outer_in[m].astype(jnp.float32)
+            in_copy(m, k).wait_recv()
+            final[m] = (left + inner_in[k].astype(jnp.float32)).astype(jnp.bfloat16)
+            fin_in_copy(m, k).start()
+            fin_out_copy(m, outer).start()
+            consume(m)
+
+            @pl.when(k > 0)
+            def _():
+                forward(k - 1)
+
+        forward(half - 1)
+
+        @pl.loop(0, half)
+        def _(k):
+            in_copy(other + k, k).wait_send()
+            fin_in_copy(mine + k, k).wait_send()
+
+        @pl.loop(0, PIECES)
+        def _(p):
+            fin_out_copy(p, outer).wait_send()
+
+    panel_ref[...] = total[...].astype(jnp.bfloat16)
+
+
+def image_step(error, moment, step):
+    rows, cols = error.shape
+    rank = moment.shape[1]
+    size, half = rows // PIECES, PIECES // 2
+    dma = pltpu.SemaphoreType.DMA
+    vmem = pl.BlockSpec(memory_space=pltpu.VMEM)
+    return pl.pallas_call(
+        image_kernel,
+        in_specs=[vmem, vmem],
+        out_specs=[vmem, vmem, vmem],
+        out_shape=[
+            jax.ShapeDtypeStruct((rows, rank), jnp.bfloat16),
+            jax.ShapeDtypeStruct((rank, cols), jnp.bfloat16),
+            jax.ShapeDtypeStruct((rank, rank), jnp.float32),
+        ],
+        scratch_shapes=[
+            pltpu.VMEM((PIECES, size, rank), jnp.bfloat16),
+            pltpu.VMEM((PIECES, size, rank), jnp.bfloat16),
+            pltpu.VMEM((half, size, rank), jnp.bfloat16),
+            pltpu.VMEM((PIECES, size, rank), jnp.bfloat16),
+            pltpu.VMEM((rank, cols), jnp.float32),
+            dma((PIECES,)), dma((PIECES,)), dma((half,)), dma((half,)),
+            dma((half,)), dma((PIECES,)), dma((PIECES,)),
+        ],
+        compiler_params=pltpu.CompilerParams(
+            collective_id=step, has_side_effects=True, vmem_limit_bytes=48 * 2**20
+        ),
+        cost_estimate=pl.CostEstimate(
+            flops=60 * 10**9, bytes_accessed=2 * rows * cols, transcendentals=0
+        ),
+        name="image_step",
+    )(error, moment)
+
+
+def local(dp, wt, weights, codes, scales, tokens, sketch):
     pairs = [(i, (i + s) % dp) for s in range(1, dp) for i in range(dp)]
 
     def dp_sum(part):
@@ -125,13 +284,22 @@
     rounded = None
     projected = None
     for step in range(ITERS + 1):
-        part = jnp.dot(error, moment, preferred_element_type=jnp.float32).astype(jnp.bfloat16)
-        share = lax.psum_scatter(part, "wt", scatter_dimension=0, tiled=True)
-        image = lax.all_gather(share, "wt", axis=0, tiled=True)
-        gram = dp_sum(cross(image, image))
-        panel = dp_sum(cross(error, image).astype(jnp.bfloat16))
+        if wt == 4:
+            image, panel, gram = image_step(error, moment, step)
+            start = lax.axis_index("wt") * (image.shape[0] // wt)
+            share = lax.dynamic_slice_in_dim(image, start, image.shape[0] // wt)
+        else:
+            part = jnp.dot(error, moment, preferred_element_type=jnp.float32)
+            share = lax.psum_scatter(
+                part.astype(jnp.bfloat16), "wt", scatter_dimension=0, tiled=True
+            )
+            image = lax.all_gather(share, "wt", axis=0, tiled=True)
+            gram = cross(image, image)
+            panel = cross(image, error).astype(jnp.bfloat16)
+        gram = dp_sum(gram)
+        panel = dp_sum(panel)
         inverse = inverse_factor(gram)
-        projected = dot_hi(panel, inverse, ((1,), (1,)))
+        projected = dot_hi(panel, inverse, ((0,), (1,)))
         if step < ITERS:
             rounded = projected.astype(jnp.bfloat16)
             scores = jnp.dot(tokens, rounded, preferred_element_type=jnp.float32)
@@ -150,7 +318,7 @@
         P(("groups", "dp"), None),
     )
     return jax.shard_map(
-        functools.partial(local, mesh.shape["dp"]),
+        functools.partial(local, mesh.shape["dp"], mesh.shape["wt"]),
         mesh=mesh,
         in_specs=placed,
         out_specs=(P(("groups", "lin"), ("dp", "wt"), None), P(("groups", "lin"), "wt", None)),

time: 440 us -> 376 us (0.85)
  waiting for transfers between devices: 241 us -> 73.9 us
  Pallas kernels: 92.9 us -> 248 us
  matrix products: 73.1 us -> 20.9 us
    pallas_call x0 -> x2, Pallas kernels: none -> 155 us  [image_step(): pl.pallas_call(image_kernel, in_specs=[vmem, vmem], out_specs=[vmem, vmem...]
    all_gather x2 -> x0, waiting for transfers between devices: 93.5 us -> none  [local(): image = lax.all_gather(share, 'wt', axis=0, tiled=True)]
    reduce_scatter x2 -> x0, waiting for transfers between devices: 87.9 us -> none  [local(): share = lax.psum_scatter(part, 'wt', scatter_dimension=0, tiled=True)]
    dot_general x2 -> x0, matrix products: 32.8 us -> none  [local(): jnp.dot(error, moment, preferred_element_type=jnp.float32)]
    dot_general x6 -> x2, matrix products: 31.5 us -> 7.61 us  [cross(): lax.dot_general(left, right, (((0,), (0,)), ((), ())), preferred_element_...]
    ppermute x6, waiting for transfers between devices: 22.5 us -> 36.9 us  [dp_sum(): other = lax.ppermute(part, 'dp', pairs)]
  transfers between devices with their start and end apart: 11 -> 7, of which waited for: 6 -> 4; matrix products, arithmetic and copies ran while one was open for 4% -> 1% of each run, Pallas kernels for 21% -> 25%
where the time goes in v2:
time: 376 us
  Pallas kernels  248 us (66%)
  waiting for transfers between devices  73.9 us (20%)
  matrix products  20.9 us (6%)
  between operations  14.2 us (4%)
  starting transfers between devices  8.69 us (2%)
  local copies, waits for them, and re-layouts  8.65 us (2%)
    pallas_call x2, Pallas kernels, image_step(): pl.pallas_call(image_kernel, in_specs=[vmem, vmem], out_specs=[vmem, vmem...  155 us
    pallas_call x2, Pallas kernels, inverse_factor(): pl.pallas_call(invert_kernel, out_shape=jax.ShapeDtypeStruct((n, n), jnp....  70.2 us
    psum x1, waiting for transfers between devices, local(): scores = lax.psum(scores.astype(jnp.bfloat16), 'wt')  37 us
    ppermute x6, waiting for transfers between devices, dp_sum(): other = lax.ppermute(part, 'dp', pairs)  36.9 us
    pallas_call x1, Pallas kernels, quant_error(): pl.pallas_call(error_kernel, grid=(rows // tile,), in_specs=[pl.BlockSpec...  22.7 us
    dot_general x3, matrix products, dot_hi(): lax.dot_general(left, right, (dims, ((), ())), precision=HIGHEST, preferr...  10.9 us
    ppermute x6, starting transfers between devices, dp_sum(): other = lax.ppermute(part, 'dp', pairs)  8.65 us
    unnamed x13, local copies, waits for them, and re-layouts  8.65 us
  transfers between devices with their start and end apart: 7, of which 4 were waited for; matrix products, arithmetic and copies ran while one was open for 1% of the time, Pallas kernels for 25%

profile of v2, /device:TPU:0, one launch (start us, length us, event | category | flops | bytes accessed | tf_op | source)
XLA Modules:
  0.0 376.1 jit_solution(16214960102424503332)
XLA Ops:
  7.2 0.0 copy-start
  7.2 0.0 copy-start.4
  7.2 0.0 all-reduce.2.cloned.1.call-start
  7.2 1.0 copy-done
  8.2 3.5 convolution_convert_fusion.2
  11.7 3.0 collective-permute-start
  14.7 0.0 copy-done.4
  14.7 0.6 copy.7
  15.3 22.7 %quant_error.1.e_ref = bf16[4096,2048]{1,0:T(8,128)(2,1)S(1)} custom-call(bf16[4096,2048]{1,0:T(8,128)(2,1)} %bitcast.23, s32[4096,2048]{1,0:T(8,128)} %bitcast.22, f32[4096,16]{1,0:T(8,128)S(1)} %bitcast.21), custom_call_target="tpu_custom_call" | custom-call | flops 33554432 | bytes 67108864 | tf_op jit(solution)/shard_map/quant_error/pallas_call | solution.py:34
  38.1 0.0 copy-start.2
  38.1 5.7 %copy-done.2 = bf16[4096,2048]{1,0:T(8,128)(2,1)} copy-done((bf16[4096,2048]{1,0:T(8,128)(2,1)}, bf16[4096,2048]{1,0:T(8,128)(2,1)S(1)}, u32[]{:S(2)}) %copy-start.2) | copy-done | bytes 16777240
  43.8 0.0 collective-permute-done
  43.8 1.5 add_convert_fusion.1.m_ref
  45.3 80.2 %image_step.2 = (bf16[4096,256]{1,0:T(8,128)(2,1)}, bf16[256,2048]{1,0:T(8,128)(2,1)S(1)}, f32[256,256]{1,0:T(8,128)S(1)}) custom-call(bf16[4096,2048]{1,0:T(8,128)(2,1)} %copy-done.2, bf16[2048,256]{1,0:T(8,128)(2,1)S(1)} %add_convert_fusion.1.m_ref), custom_call_target="tpu_custom_call" | custom-call | flops 60000002048 | bytes 16777216 | tf_op jit(solution)/shard_map/image_step/pallas_call | solution.py:241
  125.5 0.6 collective-permute-start.2
  126.1 1.5 collective-permute-start.1
  127.6 7.2 %collective-permute-done.2 = f32[256,256]{1,0:T(8,128)S(1)} collective-permute-done((f32[256,256]{1,0:T(8,128)S(1)}, f32[256,256]{1,0:T(8,128)S(1)}, u32[]{:S(2)}, u32[]{:S(2)}) %collective-permute-start.2) | collective-permute-done | bytes 262176 | tf_op jit(solution)/shard_map/ppermute | solution.py:274
  134.9 0.0 copy-start.5
  134.9 35.1 %inverse_factor.2 = f32[256,256]{1,0:T(8,128)S(1)} custom-call(f32[256,256]{1,0:T(8,128)S(1)} %add.25.a_ref), custom_call_target="tpu_custom_call" | custom-call | flops 40000000000 | bytes 524288 | tf_op jit(solution)/shard_map/inverse_factor/pallas_call | solution.py:99
  170.0 0.0 collective-permute-done.1
  170.0 3.5 convolution_convert_fusion
  173.5 0.0 copy-done.5
  173.5 2.3 fusion.7
  175.8 0.0 all-reduce.2.cloned.1.call-update
  175.9 37.0 %all-reduce.2.cloned.1.call-done = bf16[1024,256]{0,1:T(8,128)(2,1)} async-done(((bf16[1024,256]{0,1:T(8,128)(2,1)}), bf16[1024,256]{0,1:T(8,128)(2,1)}) %all-reduce.2.cloned.1.call-update) | async-done | bytes 524304 | tf_op jit(solution)/shard_map/psum | solution.py:306
  212.9 4.1 %fusion = bf16[2048,256]{1,0:T(8,128)(2,1)S(1)} fusion(bf16[1024,256]{0,1:T(8,128)(2,1)} %all-reduce.2.cloned.1.call-done, bf16[1024,2048]{1,0:T(8,128)(2,1)} %param.8), kind=kOutput, calls=%fused_computation.4 | convolution fusion | flops 1074266112 | bytes 5767168 | tf_op jit(solution)/shard_map/dot_general | solution.py:18
  217.0 1.5 collective-permute-start.3
  218.5 22.5 %collective-permute-done.3 = bf16[2048,256]{1,0:T(8,128)(2,1)S(1)} collective-permute-done((bf16[2048,256]{1,0:T(8,128)(2,1)S(1)}, bf16[2048,256]{1,0:T(8,128)(2,1)S(1)}, u32[]{:S(2)}, u32[]{:S(2)}) %collective-permute-start.3) | collective-permute-done | bytes 1048608 | tf_op jit(solution)/shard_map/ppermute | solution.py:274
  241.0 0.3 add_convert_fusion.m_ref
  241.3 74.8 %image_step.3 = (bf16[4096,256]{1,0:T(8,128)(2,1)S(1)}, bf16[256,2048]{1,0:T(8,128)(2,1)S(1)}, f32[256,256]{1,0:T(8,128)S(1)}) custom-call(bf16[4096,2048]{1,0:T(8,128)(2,1)} %copy-done.2, bf16[2048,256]{1,0:T(8,128)(2,1)S(1)} %add_convert_fusion.m_ref), custom_call_target="tpu_custom_call" | custom-call | flops 60000002048 | bytes 16777216 | tf_op jit(solution)/shard_map/image_step/pallas_call | solution.py:241
  316.0 0.0 copy-start.3
  316.0 1.3 copy-done.3
  317.4 1.9 collective-permute-start.4
  319.3 0.1 collective-permute-start.5
  319.4 7.2 %collective-permute-done.4 = f32[256,256]{1,0:T(8,128)S(1)} collective-permute-done((f32[256,256]{1,0:T(8,128)S(1)}, f32[256,256]{1,0:T(8,128)S(1)}, u32[]{:S(2)}, u32[]{:S(2)}) %collective-permute-start.4) | collective-permute-done | bytes 262176 | tf_op jit(solution)/shard_map/ppermute | solution.py:274
  326.6 35.1 %inverse_factor.3 = f32[256,256]{1,0:T(8,128)S(1)} custom-call(f32[256,256]{1,0:T(8,128)S(1)} %add.28.a_ref), custom_call_target="tpu_custom_call" | custom-call | flops 40000000000 | bytes 524288 | tf_op jit(solution)/shard_map/inverse_factor/pallas_call | solution.py:99
  361.8 0.0 copy-start.1
  361.8 2.7 convolution_bitcast_fusion.1
  364.5 0.0 collective-permute-done.5
  364.5 4.8 %convolution_bitcast_fusion = f32[1,2048,256]{2,1,0:T(8,128)} fusion(f32[256,256]{1,0:T(8,128)S(1)} %inverse_factor.3, bf16[256,2048]{1,0:T(8,128)(2,1)S(1)} %collective-permute-done.5, bf16[256,2048]{1,0:T(8,128)(2,1)S(1)} %get-tuple-element.11), kind=kOutput, calls=%fused_computation | convolution fusion | flops 1612185600 | bytes 4456448 | tf_op jit(solution)/shard_map/dot_general | solution.py:79
  369.3 0.0 copy-done.1
  (2 shorter events, 0.1 us)
Async XLA Ops:
  7.2 1.1 copy-start
  7.2 7.6 %copy-start.4 = (f32[1,16,4096]{2,1,0:T(8,128)S(1)}, f32[1,16,4096]{2,1,0:T(8,128)}, u32[]{:S(2)}) copy-start(f32[1,16,4096]{2,1,0:T(8,128)} %param.7) | copy-start | bytes 786436
  7.2 205.7 %all-reduce.2.cloned.1.call-start = ((), (), s32[]{:S(2)}) async-start(), calls=%async_computation | async-start | bytes 1048576 | tf_op jit(solution)/shard_map/psum | solution.py:306
  11.7 32.1 %collective-permute-start = (bf16[2048,256]{1,0:T(8,128)(2,1)S(1)}, bf16[2048,256]{1,0:T(8,128)(2,1)}, u32[]{:S(2)}, u32[]{:S(2)}) collective-permute-start(bf16[2048,256]{1,0:T(8,128)(2,1)S(1)} %convolution_convert_fusion.2), channel_id=1, source_target_pairs={{0,2},{2,0},{1,3},{3,1},{4,6},{6,4},{5,7},{7,5},{8,10},{10,8},{9,1... | collective-permute-start | bytes 3145736 | tf_op jit(solution)/shard_map/ppermute | solution.py:274
  38.1 5.7 %copy-start.2 = (bf16[4096,2048]{1,0:T(8,128)(2,1)}, bf16[4096,2048]{1,0:T(8,128)(2,1)S(1)}, u32[]{:S(2)}) copy-start(bf16[4096,2048]{1,0:T(8,128)(2,1)S(1)} %quant_error.1.e_ref) | copy-start | bytes 50331652
  125.5 9.3 %collective-permute-start.2 = (f32[256,256]{1,0:T(8,128)S(1)}, f32[256,256]{1,0:T(8,128)S(1)}, u32[]{:S(2)}, u32[]{:S(2)}) collective-permute-start(f32[256,256]{1,0:T(8,128)S(1)} %get-tuple-element.8), channel_id=1, source_target_pairs={{0,2},{2,0},{1,3},{3,1},{4,6},{6,4},{5,7},{7,5},{8,10},{10,8},{9,1... | collective-permute-start | bytes 786440 | tf_op jit(solution)/shard_map/ppermute | solution.py:274
  126.1 43.9 %collective-permute-start.1 = (bf16[256,2048]{1,0:T(8,128)(2,1)S(1)}, bf16[256,2048]{1,0:T(8,128)(2,1)S(1)}, u32[]{:S(2)}, u32[]{:S(2)}) collective-permute-start(bf16[256,2048]{1,0:T(8,128)(2,1)S(1)} %get-tuple-element.7), channel_id=1, source_target_pairs={{0,2},{2,0},{1,3},{3,1},{4,6},{6,4},{5,7},{7,5},{8,10},{10,8},{9,1... | collective-permute-start | bytes 3145736 | tf_op jit(solution)/shard_map/ppermute | solution.py:274
  134.9 38.6 %copy-start.5 = (bf16[1024,2048]{1,0:T(8,128)(2,1)S(1)}, bf16[1024,2048]{1,0:T(8,128)(2,1)}, u32[]{:S(2)}) copy-start(bf16[1024,2048]{1,0:T(8,128)(2,1)} %param.8) | copy-start | bytes 12582916
  217.0 24.0 %collective-permute-start.3 = (bf16[2048,256]{1,0:T(8,128)(2,1)S(1)}, bf16[2048,256]{1,0:T(8,128)(2,1)S(1)}, u32[]{:S(2)}, u32[]{:S(2)}) collective-permute-start(bf16[2048,256]{1,0:T(8,128)(2,1)S(1)} %fusion), channel_id=1, source_target_pairs={{0,2},{2,0},{1,3},{3,1},{4,6},{6,4},{5,7},{7,5},{8,10},{10,8},{9,1... | collective-permute-start | bytes 3145736 | tf_op jit(solution)/shard_map/ppermute | solution.py:274
  316.0 1.3 copy-start.3
  317.4 9.2 %collective-permute-start.4 = (f32[256,256]{1,0:T(8,128)S(1)}, f32[256,256]{1,0:T(8,128)S(1)}, u32[]{:S(2)}, u32[]{:S(2)}) collective-permute-start(f32[256,256]{1,0:T(8,128)S(1)} %get-tuple-element.10), channel_id=1, source_target_pairs={{0,2},{2,0},{1,3},{3,1},{4,6},{6,4},{5,7},{7,5},{8,10},{10,8},{9,1... | collective-permute-start | bytes 786440 | tf_op jit(solution)/shard_map/ppermute | solution.py:274
  319.3 45.2 %collective-permute-start.5 = (bf16[256,2048]{1,0:T(8,128)(2,1)S(1)}, bf16[256,2048]{1,0:T(8,128)(2,1)S(1)}, u32[]{:S(2)}, u32[]{:S(2)}) collective-permute-start(bf16[256,2048]{1,0:T(8,128)(2,1)S(1)} %get-tuple-element.11), channel_id=1, source_target_pairs={{0,2},{2,0},{1,3},{3,1},{4,6},{6,4},{5,7},{7,5},{8,10},{10,8},{9,1... | collective-permute-start | bytes 3145736 | tf_op jit(solution)/shard_map/ppermute | solution.py:274
  361.8 7.5 %copy-start.1 = (bf16[1024,256]{1,0:T(8,128)(2,1)S(1)}, bf16[1024,256]{1,0:T(8,128)(2,1)}, u32[]{:S(2)}) copy-start(bf16[1024,256]{1,0:T(8,128)(2,1)} %param.9) | copy-start | bytes 1572868
Sparse Core Ops, SparseCore 0:
  176.0 36.8 all-reduce.1

commit v3 on v2

--- a/solution.py
+++ b/solution.py
@@ -116,8 +116,9 @@
     s_part, r_outer, s_in, r_in, s_fin_in, s_fin_out, r_fin,
 ):
     me = lax.axis_index("wt")
-    half = PIECES // 2
-    size = e_ref.shape[0] // PIECES
+    pieces = stage.shape[0]
+    half = pieces // 2
+    size = e_ref.shape[0] // pieces
     low = me < 2
     is_end = (me == 0) | (me == 3)
     middle = jnp.where(low, 1, 2)
@@ -170,19 +171,19 @@
         greet(middle)
         pl.semaphore_wait(barrier, 1)
 
-        @pl.loop(0, PIECES)
+        @pl.loop(0, pieces)
         def _(t):
             p = jnp.where(lax.rem(t, 2) == 0, other, mine) + lax.div(t, 2)
             stage[p] = own(p).astype(jnp.bfloat16)
             part_copy(p).start()
 
-        @pl.loop(0, PIECES)
+        @pl.loop(0, pieces)
         def _(t):
             p = jnp.where(lax.rem(t, 2) == 0, mine, other) + lax.div(t, 2)
             fin_out_copy(p, middle).wait_recv()
             consume(p)
 
-        @pl.loop(0, PIECES)
+        @pl.loop(0, pieces)
         def _(p):
             part_copy(p).wait_send()
 
@@ -225,17 +226,17 @@
             in_copy(other + k, k).wait_send()
             fin_in_copy(mine + k, k).wait_send()
 
-        @pl.loop(0, PIECES)
+        @pl.loop(0, pieces)
         def _(p):
             fin_out_copy(p, outer).wait_send()
 
     panel_ref[...] = total[...].astype(jnp.bfloat16)
 
 
-def image_step(error, moment, step):
+def image_step(error, moment, step, pieces):
     rows, cols = error.shape
     rank = moment.shape[1]
-    size, half = rows // PIECES, PIECES // 2
+    size, half = rows // pieces, pieces // 2
     dma = pltpu.SemaphoreType.DMA
     vmem = pl.BlockSpec(memory_space=pltpu.VMEM)
     return pl.pallas_call(
@@ -248,13 +249,13 @@
             jax.ShapeDtypeStruct((rank, rank), jnp.float32),
         ],
         scratch_shapes=[
-            pltpu.VMEM((PIECES, size, rank), jnp.bfloat16),
-            pltpu.VMEM((PIECES, size, rank), jnp.bfloat16),
+            pltpu.VMEM((pieces, size, rank), jnp.bfloat16),
+            pltpu.VMEM((pieces, size, rank), jnp.bfloat16),
             pltpu.VMEM((half, size, rank), jnp.bfloat16),
-            pltpu.VMEM((PIECES, size, rank), jnp.bfloat16),
+            pltpu.VMEM((pieces, size, rank), jnp.bfloat16),
             pltpu.VMEM((rank, cols), jnp.float32),
-            dma((PIECES,)), dma((PIECES,)), dma((half,)), dma((half,)),
-            dma((half,)), dma((PIECES,)), dma((PIECES,)),
+            dma((pieces,)), dma((pieces,)), dma((half,)), dma((half,)),
+            dma((half,)), dma((pieces,)), dma((pieces,)),
         ],
         compiler_params=pltpu.CompilerParams(
             collective_id=step, has_side_effects=True, vmem_limit_bytes=48 * 2**20
@@ -285,7 +286,7 @@
     projected = None
     for step in range(ITERS + 1):
         if wt == 4:
-            image, panel, gram = image_step(error, moment, step)
+            image, panel, gram = image_step(error, moment, step, PIECES)
             start = lax.axis_index("wt") * (image.shape[0] // wt)
             share = lax.dynamic_slice_in_dim(image, start, image.shape[0] // wt)
         else:
@@ -302,9 +303,13 @@
         projected = dot_hi(panel, inverse, ((0,), (1,)))
         if step < ITERS:
             rounded = projected.astype(jnp.bfloat16)
-            scores = jnp.dot(tokens, rounded, preferred_element_type=jnp.float32)
-            scores = lax.psum(scores.astype(jnp.bfloat16), "wt")
-            moment = token_moment(scores)
+            if wt == 4:
+                _, part, _ = image_step(tokens, rounded, ITERS + 1 + step, PIECES // 2)
+                moment = dp_sum(part).T.astype(jnp.bfloat16)
+            else:
+                scores = jnp.dot(tokens, rounded, preferred_element_type=jnp.float32)
+                scores = lax.psum(scores.astype(jnp.bfloat16), "wt")
+                moment = token_moment(scores)
     basis = dot_hi(share.astype(jnp.float32), inverse * math.sqrt(OUT), ((1,), (1,)))
     return (basis[None], projected[None])
 

time: 376 us -> 337 us (0.90)
  waiting for transfers between devices: 73.9 us -> 25.8 us
  Pallas kernels: 248 us -> 277 us
  between operations: 14.2 us -> 0.77 us
  matrix products: 20.9 us -> 14.4 us
    psum x1 -> x0, waiting for transfers between devices: 37 us -> none  [local(): scores = lax.psum(scores.astype(jnp.bfloat16), 'wt')]
    pallas_call x2 -> x3, Pallas kernels: 155 us -> 184 us  [image_step(): pl.pallas_call(image_kernel, in_specs=[vmem, vmem], out_specs=[vmem, vmem...]
    ppermute x6, waiting for transfers between devices: 36.9 us -> 25.8 us  [dp_sum(): other = lax.ppermute(part, 'dp', pairs)]
    dot_general x2 -> x1, matrix products: 7.61 us -> 3.51 us  [cross(): lax.dot_general(left, right, (((0,), (0,)), ((), ())), preferred_element_...]
    unnamed x13 -> x11, local copies, waits for them, and re-layouts: 8.65 us -> 8.68 us
  transfers between devices with their start and end apart: 7 -> 6, of which waited for: 4 -> 3; matrix products, arithmetic and copies ran while one was open for 1% -> 1% of each run, Pallas kernels for 25% -> 28%
where the time goes in v3:
time: 337 us
  Pallas kernels  277 us (82%)
  waiting for transfers between devices  25.8 us (8%)
  matrix products  14.4 us (4%)
  local copies, waits for them, and re-layouts  9.2 us (3%)
  starting transfers between devices  7.71 us (2%)
    pallas_call x3, Pallas kernels, image_step(): pl.pallas_call(image_kernel, in_specs=[vmem, vmem], out_specs=[vmem, vmem...  184 us
    pallas_call x2, Pallas kernels, inverse_factor(): pl.pallas_call(invert_kernel, out_shape=jax.ShapeDtypeStruct((n, n), jnp....  70.2 us
    ppermute x6, waiting for transfers between devices, dp_sum(): other = lax.ppermute(part, 'dp', pairs)  25.8 us
    pallas_call x1, Pallas kernels, quant_error(): pl.pallas_call(error_kernel, grid=(rows // tile,), in_specs=[pl.BlockSpec...  22.7 us
    dot_general x3, matrix products, dot_hi(): lax.dot_general(left, right, (dims, ((), ())), precision=HIGHEST, preferr...  10.9 us
    unnamed x11, local copies, waits for them, and re-layouts  8.68 us
    ppermute x6, starting transfers between devices, dp_sum(): other = lax.ppermute(part, 'dp', pairs)  7.71 us
  transfers between devices with their start and end apart: 6, of which 3 were waited for; matrix products, arithmetic and copies ran while one was open for 1% of the time, Pallas kernels for 28%

profile of v3, /device:TPU:0, one launch (start us, length us, event | category | flops | bytes accessed | tf_op | source)
XLA Modules:
  0.0 337.0 jit_solution(12999440306614038093)
XLA Ops:
  0.6 0.0 copy-start
  0.6 0.0 copy-start.4
  0.7 1.0 copy-done
  1.7 3.5 %convolution_convert_fusion.1 = bf16[2048,256]{1,0:T(8,128)(2,1)S(1)} fusion(bf16[1024,2048]{1,0:T(8,128)(2,1)} %e_ref.1, bf16[1024,256]{1,0:T(8,128)(2,1)S(1)} %copy-done), kind=kOutput, calls=%fused_computation.2 | convolution fusion | flops 1074266112 | bytes 5767168 | tf_op jit(solution)/shard_map/dot_general | solution.py:18
  5.2 3.0 collective-permute-start
  8.2 0.0 copy-done.4
  8.2 0.6 copy.7
  8.8 22.7 %quant_error.1.e_ref = bf16[4096,2048]{1,0:T(8,128)(2,1)S(1)} custom-call(bf16[4096,2048]{1,0:T(8,128)(2,1)} %bitcast.17, s32[4096,2048]{1,0:T(8,128)} %bitcast.16, f32[4096,16]{1,0:T(8,128)S(1)} %bitcast.15), custom_call_target="tpu_custom_call" | custom-call | flops 33554432 | bytes 67108864 | tf_op jit(solution)/shard_map/quant_error/pallas_call | solution.py:34
  31.5 0.0 copy-start.2
  31.5 5.7 %copy-done.2 = bf16[4096,2048]{1,0:T(8,128)(2,1)} copy-done((bf16[4096,2048]{1,0:T(8,128)(2,1)}, bf16[4096,2048]{1,0:T(8,128)(2,1)S(1)}, u32[]{:S(2)}) %copy-start.2) | copy-done | bytes 16777240
  37.3 0.0 collective-permute-done
  37.3 1.5 add_convert_fusion.1.m_ref
  38.8 80.2 %image_step.3 = (bf16[4096,256]{1,0:T(8,128)(2,1)}, bf16[256,2048]{1,0:T(8,128)(2,1)S(1)}, f32[256,256]{1,0:T(8,128)S(1)}) custom-call(bf16[4096,2048]{1,0:T(8,128)(2,1)} %copy-done.2, bf16[2048,256]{1,0:T(8,128)(2,1)S(1)} %add_convert_fusion.1.m_ref), custom_call_target="tpu_custom_call" | custom-call | flops 60000002048 | bytes 16777216 | tf_op jit(solution)/shard_map/image_step/pallas_call | solution.py:242
  119.0 0.6 collective-permute-start.2
  119.6 1.5 collective-permute-start.1
  121.1 7.2 %collective-permute-done.2 = f32[256,256]{1,0:T(8,128)S(1)} collective-permute-done((f32[256,256]{1,0:T(8,128)S(1)}, f32[256,256]{1,0:T(8,128)S(1)}, u32[]{:S(2)}, u32[]{:S(2)}) %collective-permute-start.2) | collective-permute-done | bytes 262176 | tf_op jit(solution)/shard_map/ppermute | solution.py:275
  128.3 35.1 %inverse_factor.2 = f32[256,256]{1,0:T(8,128)S(1)} custom-call(f32[256,256]{1,0:T(8,128)S(1)} %add.23.a_ref), custom_call_target="tpu_custom_call" | custom-call | flops 40000000000 | bytes 524288 | tf_op jit(solution)/shard_map/inverse_factor/pallas_call | solution.py:99
  163.4 0.0 collective-permute-done.1
  163.5 3.4 %convolution_convert_fusion.m_ref = bf16[2048,256]{1,0:T(8,128)(2,1)S(1)} fusion(f32[256,256]{1,0:T(8,128)S(1)} %inverse_factor.2, bf16[256,2048]{1,0:T(8,128)(2,1)S(1)} %collective-permute-done.1, bf16[256,2048]{1,0:T(8,128)(2,1)S(1)} %get-tuple-element.8), kind=kOutput, calls=%fused_computation.1 | convolution fusion | flops 1612709888 | bytes 3407872 | tf_op jit(solution)/shard_map/dot_general | solution.py:79
  166.9 31.9 %image_step.4 = (bf16[1024,256]{1,0:T(8,128)(2,1)}, bf16[256,2048]{1,0:T(8,128)(2,1)S(1)}, f32[256,256]{1,0:T(8,128)}) custom-call(bf16[1024,2048]{1,0:T(8,128)(2,1)} %e_ref.1, bf16[2048,256]{1,0:T(8,128)(2,1)S(1)} %convolution_convert_fusion.m_ref), custom_call_target="tpu_custom_call" | custom-call | flops 60000002048 | bytes 4194304 | tf_op jit(solution)/shard_map/image_step/pallas_call | solution.py:242
  198.8 0.5 copy.8
  199.4 0.6 collective-permute-start.3
  200.0 14.3 %collective-permute-done.3 = bf16[256,2048]{0,1:T(8,128)(2,1)S(1)} collective-permute-done((bf16[256,2048]{0,1:T(8,128)(2,1)S(1)}, bf16[256,2048]{0,1:T(8,128)(2,1)S(1)}, u32[]{:S(2)}, u32[]{:S(2)}) %collective-permute-start.3) | collective-permute-done | bytes 1048608 | tf_op jit(solution)/shard_map/ppermute | solution.py:275
  214.2 0.3 fusion.6.m_ref
  214.5 72.2 %image_step.5 = (bf16[4096,256]{1,0:T(8,128)(2,1)S(1)}, bf16[256,2048]{1,0:T(8,128)(2,1)S(1)}, f32[256,256]{1,0:T(8,128)S(1)}) custom-call(bf16[4096,2048]{1,0:T(8,128)(2,1)} %copy-done.2, bf16[2048,256]{1,0:T(8,128)(2,1)S(1)} %fusion.6.m_ref), custom_call_target="tpu_custom_call" | custom-call | flops 60000002048 | bytes 16777216 | tf_op jit(solution)/shard_map/image_step/pallas_call | solution.py:242
  286.7 0.0 copy-start.3
  286.7 1.3 copy-done.3
  288.0 0.6 collective-permute-start.4
  288.6 1.5 collective-permute-start.5
  290.0 4.3 %collective-permute-done.4 = f32[256,256]{1,0:T(8,128)S(1)} collective-permute-done((f32[256,256]{1,0:T(8,128)S(1)}, f32[256,256]{1,0:T(8,128)S(1)}, u32[]{:S(2)}, u32[]{:S(2)}) %collective-permute-start.4) | collective-permute-done | bytes 262176 | tf_op jit(solution)/shard_map/ppermute | solution.py:275
  294.4 35.1 %inverse_factor.3 = f32[256,256]{1,0:T(8,128)S(1)} custom-call(f32[256,256]{1,0:T(8,128)S(1)} %add.26.a_ref), custom_call_target="tpu_custom_call" | custom-call | flops 40000000000 | bytes 524288 | tf_op jit(solution)/shard_map/inverse_factor/pallas_call | solution.py:99
  329.5 0.0 copy-start.1
  329.5 2.7 convolution_bitcast_fusion.1
  332.2 0.0 collective-permute-done.5
  332.2 4.8 %convolution_bitcast_fusion = f32[1,2048,256]{2,1,0:T(8,128)} fusion(f32[256,256]{1,0:T(8,128)S(1)} %inverse_factor.3, bf16[256,2048]{1,0:T(8,128)(2,1)S(1)} %collective-permute-done.5, bf16[256,2048]{1,0:T(8,128)(2,1)S(1)} %get-tuple-element.13), kind=kOutput, calls=%fused_computation | convolution fusion | flops 1612185600 | bytes 4456448 | tf_op jit(solution)/shard_map/dot_general | solution.py:79
  337.0 0.0 copy-done.1
  (2 shorter events, 0.1 us)
Async XLA Ops:
  0.6 1.1 copy-start
  0.6 7.6 %copy-start.4 = (f32[1,16,4096]{2,1,0:T(8,128)S(1)}, f32[1,16,4096]{2,1,0:T(8,128)}, u32[]{:S(2)}) copy-start(f32[1,16,4096]{2,1,0:T(8,128)} %param.7) | copy-start | bytes 786436
  5.2 32.1 %collective-permute-start = (bf16[2048,256]{1,0:T(8,128)(2,1)S(1)}, bf16[2048,256]{1,0:T(8,128)(2,1)}, u32[]{:S(2)}, u32[]{:S(2)}) collective-permute-start(bf16[2048,256]{1,0:T(8,128)(2,1)S(1)} %convolution_convert_fusion.1), channel_id=1, source_target_pairs={{0,2},{2,0},{1,3},{3,1},{4,6},{6,4},{5,7},{7,5},{8,10},{10,8},{9,1... | collective-permute-start | bytes 3145736 | tf_op jit(solution)/shard_map/ppermute | solution.py:275
  31.5 5.7 %copy-start.2 = (bf16[4096,2048]{1,0:T(8,128)(2,1)}, bf16[4096,2048]{1,0:T(8,128)(2,1)S(1)}, u32[]{:S(2)}) copy-start(bf16[4096,2048]{1,0:T(8,128)(2,1)S(1)} %quant_error.1.e_ref) | copy-start | bytes 50331652
  119.0 9.3 %collective-permute-start.2 = (f32[256,256]{1,0:T(8,128)S(1)}, f32[256,256]{1,0:T(8,128)S(1)}, u32[]{:S(2)}, u32[]{:S(2)}) collective-permute-start(f32[256,256]{1,0:T(8,128)S(1)} %get-tuple-element.9), channel_id=1, source_target_pairs={{0,2},{2,0},{1,3},{3,1},{4,6},{6,4},{5,7},{7,5},{8,10},{10,8},{9,1... | collective-permute-start | bytes 786440 | tf_op jit(solution)/shard_map/ppermute | solution.py:275
  119.6 43.9 %collective-permute-start.1 = (bf16[256,2048]{1,0:T(8,128)(2,1)S(1)}, bf16[256,2048]{1,0:T(8,128)(2,1)S(1)}, u32[]{:S(2)}, u32[]{:S(2)}) collective-permute-start(bf16[256,2048]{1,0:T(8,128)(2,1)S(1)} %get-tuple-element.8), channel_id=1, source_target_pairs={{0,2},{2,0},{1,3},{3,1},{4,6},{6,4},{5,7},{7,5},{8,10},{10,8},{9,1... | collective-permute-start | bytes 3145736 | tf_op jit(solution)/shard_map/ppermute | solution.py:275
  199.4 14.9 %collective-permute-start.3 = (bf16[256,2048]{0,1:T(8,128)(2,1)S(1)}, bf16[256,2048]{0,1:T(8,128)(2,1)S(1)}, u32[]{:S(2)}, u32[]{:S(2)}) collective-permute-start(bf16[256,2048]{0,1:T(8,128)(2,1)S(1)} %copy.8), channel_id=1, source_target_pairs={{0,2},{2,0},{1,3},{3,1},{4,6},{6,4},{5,7},{7,5},{8,10},{10,8},{9,1... | collective-permute-start | bytes 3145736 | tf_op jit(solution)/shard_map/ppermute | solution.py:275
  286.7 1.3 copy-start.3
  288.0 6.4 %collective-permute-start.4 = (f32[256,256]{1,0:T(8,128)S(1)}, f32[256,256]{1,0:T(8,128)S(1)}, u32[]{:S(2)}, u32[]{:S(2)}) collective-permute-start(f32[256,256]{1,0:T(8,128)S(1)} %get-tuple-element.12), channel_id=1, source_target_pairs={{0,2},{2,0},{1,3},{3,1},{4,6},{6,4},{5,7},{7,5},{8,10},{10,8},{9,1... | collective-permute-start | bytes 786440 | tf_op jit(solution)/shard_map/ppermute | solution.py:275
  288.6 43.7 %collective-permute-start.5 = (bf16[256,2048]{1,0:T(8,128)(2,1)S(1)}, bf16[256,2048]{1,0:T(8,128)(2,1)S(1)}, u32[]{:S(2)}, u32[]{:S(2)}) collective-permute-start(bf16[256,2048]{1,0:T(8,128)(2,1)S(1)} %get-tuple-element.13), channel_id=1, source_target_pairs={{0,2},{2,0},{1,3},{3,1},{4,6},{6,4},{5,7},{7,5},{8,10},{10,8},{9,1... | collective-permute-start | bytes 3145736 | tf_op jit(solution)/shard_map/ppermute | solution.py:275
  329.5 7.5 %copy-start.1 = (bf16[1024,256]{1,0:T(8,128)(2,1)S(1)}, bf16[1024,256]{1,0:T(8,128)(2,1)}, u32[]{:S(2)}) copy-start(bf16[1024,256]{1,0:T(8,128)(2,1)} %param.9) | copy-start | bytes 1572868
